TPU v7x, 512 devices: a whole 4x4x16 slice. The times are simulated.
512 devices in a mesh: dp: 64 (over z, x_hi, core), head: 8 (over y, x_lo).
Axes of the slice: x: 4 (x_hi: 2, x_lo: 2; x = x_hi * 2 + x_lo), y: 4, z: 16, core: 2. Of those that a mesh axis runs over, the one named last changes fastest.
Arguments:
- query_clean: float32 [16384, 8192], P(('dp', 'head')), may hold values from -320 to 320
- key_clean: float32 [16384, 1024], P(('dp', 'head')), may hold values from -12 to 12
- clean_value_rows: float32 [16384, 1024], P(('dp', 'head')), may hold values from -6 to 6
- query_corrupt: float32 [16384, 8192], P(('dp', 'head')), may hold values from -320 to 320
- key_corrupt: float32 [16384, 1024], P(('dp', 'head')), may hold values from -12 to 12
- corrupted_value_rows: float32 [16384, 1024], P(('dp', 'head')), may hold values from -6 to 6
- cotangent: float32 [16384, 8192], P(('dp', 'head')), may hold values from -0.3 to 0.3
- bin_segments: int32 [64, 256], P('dp'), may hold values from 0 to 3, never falling along the last dimension, each value on 1 to 128 neighbouring positions
- plan: int32 [64, 64], P('dp'), may hold values from 0 to 63, each once within a row
- offsets: int32 [64], replicated, may hold values from 0 to 63, each once
Outputs:
- head_scores: float32 [256, 64], P('dp', 'head')
- query_scores: float32 [256, 64], P('dp', 'head')
- kv_scores: float32 [256, 8], P('dp', 'head')
Inputs may be any that keep to these rules, and one draw needn't show every extreme that they name: `plan`: each row is a permutation of 0 to 63. `offsets`: a permutation: every bin receives exactly one block from each dp index.
All inputs are finite; a program needn't handle non-finite values.
Results may differ from a plain program's by a relative error of at most 0.0003.
Values sent between devices are 32-bit elements; how exact they have to be, the bound alone decides.
A program may use at most 64 MiB of HBM per device.

v0:
```python
import functools

import jax
import jax.numpy as jnp
from jax import lax
from jax.experimental import pallas as pl
from jax.experimental.pallas import tpu as pltpu
from jax.sharding import PartitionSpec as P

MESH = pl.DeviceIdType.MESH
F32 = jnp.float32
BF16 = jnp.bfloat16
HEAD_SIZE = 128
PAIRS_PER_BIN = 4
ROWS = 4
SUB = 4
CHUNKS = 4


def iota(shape, dim):
    return lax.broadcasted_iota(jnp.int32, shape, dim)


def split3(x):
    high = x.astype(BF16)
    rest = x - high.astype(F32)
    middle = rest.astype(BF16)
    low = (rest - middle.astype(F32)).astype(BF16)
    return high, middle, low


def left_terms(x):
    high, middle, low = split3(x)
    return jnp.concatenate([high, middle, high, middle, high, low], axis=1)


def right_terms(x):
    high, middle, low = split3(x)
    return jnp.concatenate([high, middle, middle, high, low, high], axis=1)


def product(left, right):
    return lax.dot_general(left, right, (((1,), (1,)), ((), ())), preferred_element_type=F32)


def kernel(
    n, heads, group,
    query, key, value, query_other, key_other, value_other, cotangent, segments, plan, offsets,
    head_out, query_out, kv_out,
    first_kv, first_q, send_kv, send_q, bin_kv, bin_q,
    key_terms, value_terms, bias, sums, loose, segments_other, part_out, part_in,
    send1, recv1, send2, recv2, small_send, small_recv,
):
    me = lax.axis_index("dp")
    head = lax.axis_index("head")
    half = n // 2
    ring = n // SUB
    width = HEAD_SIZE
    rows_here = ROWS * n // heads
    per_chunk = group // CHUNKS
    chunk_width = per_chunk * width
    z, sub = me // SUB, me % SUB
    odd_core = sub % 2
    pair = me % half
    own_bit = me // half
    partner = (me + half) % n

    barrier = pltpu.get_barrier_semaphore()

    def greet_dp(i, carry):
        pl.semaphore_signal(barrier, inc=1, device_id=((me + i) % n, head), device_id_type=MESH)
        return carry

    def greet_head(i, carry):
        pl.semaphore_signal(barrier, inc=1, device_id=(me, (head + i) % heads), device_id_type=MESH)
        return carry

    lax.fori_loop(1, heads, greet_head, 0)
    lax.fori_loop(1, n, greet_dp, 0)
    pl.semaphore_wait(barrier, n - 1 + heads - 1)

    def sources(chunk, j):
        if chunk == 0:
            for place, ref in enumerate((key, value, key_other, value_other)):
                yield ref, pl.multiple_of(j * width, width), width, place * width
        else:
            begin = (chunk - 1) * chunk_width
            for place, ref in enumerate((query, query_other, cotangent)):
                at = pl.multiple_of(j * (group * width) + begin, width)
                yield ref, at, chunk_width, place * chunk_width

    def first_of(chunk):
        return first_kv if chunk == 0 else first_q.at[chunk - 1]

    def send_of(chunk):
        return send_kv if chunk == 0 else send_q.at[chunk - 1]

    def bin_of(chunk):
        return bin_kv if chunk == 0 else bin_q.at[chunk - 1]

    def start_first(chunk):
        at = pl.multiple_of(head * rows_here, 8)

        def to(i, carry):
            j = (head + i) % heads
            for ref, column, columns, place in sources(chunk, j):
                pltpu.make_async_remote_copy(
                    src_ref=ref.at[:, pl.ds(column, columns)],
                    dst_ref=first_of(chunk).at[pl.ds(at, rows_here), pl.ds(place, columns)],
                    send_sem=send1.at[chunk],
                    recv_sem=recv1.at[chunk],
                    device_id=(me, j),
                    device_id_type=MESH,
                ).start()
            return carry

        lax.fori_loop(1, heads, to, 0)
        for ref, column, columns, place in sources(chunk, head):
            pltpu.make_async_copy(
                ref.at[:, pl.ds(column, columns)],
                first_of(chunk).at[pl.ds(at, rows_here), pl.ds(place, columns)],
                recv1.at[chunk],
            ).start()

    def wait_for(ref, semaphore):
        pltpu.make_async_copy(ref, ref, semaphore).wait()

    def step_along(j, count, flipped):
        size = (count - j) // 2
        sign = (1 - 2 * (j % 2)) * (1 - 2 * flipped)
        return sign * size

    def start_second(chunk):
        count = ring if chunk == 0 else ring // 2

        def copy(t, remote):
            j, i = t // SUB, t % SUB
            z_to = (z + step_along(j, count, odd_core) + ring) % ring
            to = z_to * SUB + (sub + 1 + i) % SUB
            slot = me if chunk == 0 else j * SUB + sub
            source = send_of(chunk).at[pl.ds(pl.multiple_of(to % half * 8, 8), 8)]
            target = bin_of(chunk).at[pl.ds(pl.multiple_of(slot * 8, 8), 8)]
            if not remote:
                pltpu.make_async_copy(source, target, recv2.at[chunk]).start()
                return
            pltpu.make_async_remote_copy(
                src_ref=source,
                dst_ref=target,
                send_sem=send2.at[chunk],
                recv_sem=recv2.at[chunk],
                device_id=(to, head),
                device_id_type=MESH,
            ).start()

        def step(t, carry):
            copy(t, True)
            return carry

        last = count * SUB - 1
        lax.fori_loop(0, last, step, 0)
        copy(last, False)

    start_first(0)
    start_first(1)
    segment_copy = pltpu.make_async_remote_copy(
        src_ref=segments,
        dst_ref=segments_other,
        send_sem=small_send.at[0],
        recv_sem=small_recv.at[0],
        device_id=(partner, head),
        device_id_type=MESH,
    )
    segment_copy.start()

    off_row = offsets[...].astype(F32)
    plan_row = plan[...].astype(F32)
    square = (n, n)
    same = iota(square, 0) == iota(square, 1)
    lanes = iota(square, 1).astype(F32)
    off_column = jnp.sum(jnp.where(same, off_row, 0.0), axis=1, keepdims=True)
    plan_column = jnp.sum(jnp.where(same, plan_row, 0.0), axis=1, keepdims=True)
    distance = jnp.sum(jnp.where(plan_column == lanes, off_row, 0.0), axis=1, keepdims=True)
    target = me.astype(F32) + distance
    target = jnp.where(target >= n, target - n, target)
    wide = (n, ROWS * n)
    block = iota(wide, 1) // ROWS
    target_row = jnp.sum(jnp.where(iota(wide, 0) == block, target, 0.0), axis=0, keepdims=True)
    one = (1, ROWS * n)
    key_in = target_row * ROWS + (iota(one, 1) % ROWS).astype(F32)
    out = iota((ROWS * n, 1), 0)
    key_to = ((out // 8 + half * (out % 2)) * ROWS + out % 8 // 2).astype(F32)
    order = jnp.where(key_to == key_in, 1.0, 0.0).astype(BF16)

    def reorder(chunk):
        source, place = first_of(chunk), send_of(chunk)
        columns = 4 * width if chunk == 0 else 3 * chunk_width
        for begin in range(0, columns, 256):
            high, middle, low = split3(source[:, begin : begin + 256])
            moved = jnp.dot(order, high, preferred_element_type=F32)
            moved += jnp.dot(order, middle, preferred_element_type=F32)
            moved += jnp.dot(order, low, preferred_element_type=F32)
            place[:, begin : begin + 256] = moved

    for chunk in range(CHUNKS + 1):
        wait_for(first_of(chunk), recv1.at[chunk])
        reorder(chunk)
        start_second(chunk)
        if chunk + 2 <= CHUNKS:
            start_first(chunk + 2)

    segment_copy.wait()
    q_index = iota((half * ROWS, 1), 0)
    slot = q_index // ROWS
    slot_sub = slot % SUB
    slot_z = z - step_along(slot // SUB, ring // 2, slot_sub % 2)
    q_source = (slot_z + ring) % ring * SUB + slot_sub
    k_source = iota(one, 1) // ROWS
    members = []
    for bit in range(2):
        which = pair + bit * half
        segment = jnp.where(own_bit == bit, segments[...], segments_other[...])
        starts = [
            jnp.sum(jnp.where(segment < g, 1.0, 0.0), axis=1, keepdims=True)
            for g in range(1, PAIRS_PER_BIN)
        ]
        k_distance = ((which - k_source + n) % n).astype(F32)
        k_slot = jnp.sum(
            jnp.where(off_column == k_distance, iota(wide, 0).astype(F32), 0.0), axis=0, keepdims=True
        )
        k_place = k_slot * ROWS + (iota(one, 1) % ROWS).astype(F32)
        q_distance = ((which - q_source + n) % n).astype(F32)
        tall = (half * ROWS, n)
        q_slot = jnp.sum(
            jnp.where(off_row == q_distance, iota(tall, 1).astype(F32), 0.0), axis=1, keepdims=True
        )
        q_place = q_slot * ROWS + (q_index % ROWS).astype(F32)
        begin = jnp.zeros_like(q_place)
        k_segment = jnp.zeros_like(k_place)
        for start in starts:
            begin = jnp.where(q_place >= start, start, begin)
            k_segment += jnp.where(k_place >= start, 1.0, 0.0)
        allowed = jnp.logical_and(k_place <= q_place, k_place >= begin)
        bias[bit] = jnp.where(allowed, 0.0, -jnp.inf)
        members.append(
            jnp.where(k_segment == iota((8, ROWS * n), 0).astype(F32), 1.0, 0.0)
        )

    wait_for(bin_kv, recv2.at[0])
    keys = ROWS * n
    for place, (terms, begin) in enumerate(
        ((key_terms, 0), (value_terms, 0), (key_terms, keys), (value_terms, keys))
    ):
        loose[place] = bin_kv[:, place * width : (place + 1) * width]
        for bit in range(2):
            found = loose[place, pl.ds(bit, keys, stride=2), :]
            terms[bit, begin : begin + keys, :] = right_terms(found)

    scale = width**-0.5
    tile = (-1, 8, keys)

    def softmax(scores, mask):
        scores = scores * scale + mask
        raised = jnp.exp(scores - jnp.max(scores, axis=1, keepdims=True))
        return raised * (1.0 / jnp.sum(raised, axis=1, keepdims=True))

    sums[...] = jnp.zeros_like(sums)

    def work(c, carry):
        wait_for(bin_q.at[c], recv2.at[c + 1])
        for inner in range(per_chunk):
            for place in range(3):
                begin = place * chunk_width + inner * width
                loose[place, :keys] = bin_q[c, :, begin : begin + width]
            for bit in range(2):

                def rows(place):
                    return loose[place, pl.ds(bit, half * ROWS, stride=2), :]

                both = jnp.concatenate([left_terms(rows(0)), left_terms(rows(1))], axis=0)
                scores = product(both, key_terms[bit])
                grads = product(left_terms(rows(2)), value_terms[bit])
                top, bottom = scores[: half * ROWS], scores[half * ROWS :]
                plain = top[:, :keys]
                mask = bias[bit]
                weight = softmax(plain, mask)
                weight_other = softmax(bottom[:, keys:], mask)
                part = weight * grads[:, :keys]
                row_dot = jnp.sum(part, axis=1, keepdims=True)
                slope = (part - weight * row_dot) * scale
                head_term = weight_other * grads[:, keys:] - part
                query_term = slope * (bottom[:, :keys] - plain)
                kv_term = slope * (top[:, keys:] - plain) + (weight * grads[:, keys:] - part)
                at = c * per_chunk + inner
                sums[bit, at] = jnp.sum(head_term.reshape(tile), axis=0)
                sums[bit, group + at] = jnp.sum(query_term.reshape(tile), axis=0)
                sums[bit, 2 * group] += jnp.sum(kv_term.reshape(tile), axis=0)
        return carry

    lax.fori_loop(0, CHUNKS, work, 0)

    parts = []
    for bit in range(2):
        lines = [jnp.sum(sums[bit, i], axis=0, keepdims=True) for i in range(2 * group + 1)]
        lines.append(jnp.zeros((width - len(lines), keys), F32))
        lines = jnp.concatenate(lines, axis=0)
        parts.append(
            lax.dot_general(
                members[bit], lines, (((1,), (1,)), ((), ())),
                precision=lax.Precision.HIGHEST, preferred_element_type=F32,
            )
        )
    part_out[...] = jnp.where(own_bit == 0, parts[1], parts[0])
    exchange = pltpu.make_async_remote_copy(
        src_ref=part_out,
        dst_ref=part_in,
        send_sem=small_send.at[1],
        recv_sem=small_recv.at[1],
        device_id=(partner, head),
        device_id_type=MESH,
    )
    exchange.start()
    mine = jnp.where(own_bit == 0, parts[0], parts[1])

    for chunk in range(CHUNKS + 1):
        wait_for(first_of(chunk).at[pl.ds(0, (heads - 1) * rows_here)], send1.at[chunk])
        sent = (n if chunk == 0 else half) - 1
        wait_for(bin_of(chunk).at[pl.ds(0, sent * 8)], send2.at[chunk])

    exchange.wait()
    total = mine + part_in[...]
    head_out[...] = total[:PAIRS_PER_BIN, :group]
    query_out[...] = total[:PAIRS_PER_BIN, group : 2 * group]
    kv_out[...] = total[:PAIRS_PER_BIN, 2 * group : 2 * group + 1]


def shards(n, heads, *arrays):
    segments, plan, offsets = arrays[7:]
    group = arrays[0].shape[1] // arrays[1].shape[1]
    per_chunk = group // CHUNKS
    rows = ROWS * n
    kv_columns, q_columns = 4 * HEAD_SIZE, 3 * per_chunk * HEAD_SIZE
    hbm = pl.BlockSpec(memory_space=pltpu.HBM)
    vmem = pl.BlockSpec(memory_space=pltpu.VMEM)
    return pl.pallas_call(
        functools.partial(kernel, n, heads, group),
        out_shape=[
            jax.ShapeDtypeStruct((PAIRS_PER_BIN, group), F32),
            jax.ShapeDtypeStruct((PAIRS_PER_BIN, group), F32),
            jax.ShapeDtypeStruct((PAIRS_PER_BIN, 1), F32),
        ],
        in_specs=[hbm] * 7 + [vmem] * 3,
        out_specs=[vmem] * 3,
        scratch_shapes=[
            pltpu.VMEM((rows, kv_columns), F32),
            pltpu.VMEM((CHUNKS, rows, q_columns), F32),
            pltpu.VMEM((rows, kv_columns), F32),
            pltpu.VMEM((CHUNKS, rows, q_columns), F32),
            pltpu.VMEM((2 * rows, kv_columns), F32),
            pltpu.VMEM((CHUNKS, rows, q_columns), F32),
            pltpu.VMEM((2, 2 * rows, 6 * HEAD_SIZE), BF16),
            pltpu.VMEM((2, 2 * rows, 6 * HEAD_SIZE), BF16),
            pltpu.VMEM((2, rows // 2, rows), F32),
            pltpu.VMEM((2, 2 * group + 1, 8, rows), F32),
            pltpu.VMEM((4, 2 * rows, HEAD_SIZE), F32),
            pltpu.VMEM((1, rows), jnp.int32),
            pltpu.VMEM((8, HEAD_SIZE), F32),
            pltpu.VMEM((8, HEAD_SIZE), F32),
            pltpu.SemaphoreType.DMA((CHUNKS + 1,)),
            pltpu.SemaphoreType.DMA((CHUNKS + 1,)),
            pltpu.SemaphoreType.DMA((CHUNKS + 1,)),
            pltpu.SemaphoreType.DMA((CHUNKS + 1,)),
            pltpu.SemaphoreType.DMA((2,)),
            pltpu.SemaphoreType.DMA((2,)),
        ],
        compiler_params=pltpu.CompilerParams(
            collective_id=0, has_side_effects=True, vmem_limit_bytes=60 * 1024 * 1024
        ),
    )(*arrays[:7], segments, plan, offsets.reshape(1, -1))


def solution(mesh):
    rows = P(("dp", "head"), None)
    return jax.shard_map(
        functools.partial(shards, mesh.shape["dp"], mesh.shape["head"]),
        mesh=mesh,
        in_specs=(rows,) * 7 + (P("dp", None), P("dp", None), P()),
        out_specs=(P("dp", "head"),) * 3,
        check_vma=False,
    )
```

profile of v0, /device:TPU:1, one launch (start us, length us, event | category | flops | bytes accessed | tf_op | source)
XLA Modules:
  0.0 155.9 jit_solution(1969511413368556650)
XLA Ops:
  0.6 152.8 %shard_map.121 = (f32[4,8]{1,0:T(4,128)}, f32[4,8]{1,0:T(4,128)}, f32[4,1]{1,0:T(4,128)}) custom-call(f32[32,8192]{1,0:T(8,128)} %query.1, f32[32,1024]{1,0:T(8,128)} %key.1, f32[32,1024]{1,0:T(8,128)} %value.1, f32[32,8192]{1,0:T(8,128)} %query_other.1, f32[32,1024]{1,0:T(8,128)} %key_other.1, f32[32,1024]{1,0:T(8,128)} %value_other.1, ...), custom_call_target="tpu_custom_call" | custom-call | tf_op jit(solution)/shard_map/pallas_call | solution.py:344
  153.4 0.0 copy-start
  153.4 0.0 copy-start.2
  153.4 0.7 copy-done
  154.1 0.6 copy.13
  154.7 0.0 copy-done.2
  154.7 0.0 copy-start.1
  154.7 0.6 copy.16
  155.3 0.1 copy-done.1
  155.4 0.6 copy.17
Async XLA Ops:
  153.4 0.7 copy-start
  153.4 1.3 copy-start.2
  154.7 0.7 copy-start.1
where the time goes:
time: 156 us
  Pallas kernels  153 us (98%)
  local copies, waits for them, and re-layouts  2.51 us (2%)
    pallas_call x1, Pallas kernels, shards(): pl.pallas_call(functools.partial(kernel, n, heads, group), out_shape=[jax...  153 us

commit v1 on v0

v1 whole, which is shorter than its diff:
```python
import functools

import jax
import jax.numpy as jnp
from jax import lax
from jax.experimental import pallas as pl
from jax.experimental.pallas import tpu as pltpu
from jax.sharding import PartitionSpec as P

MESH = pl.DeviceIdType.MESH
F32 = jnp.float32
BF16 = jnp.bfloat16
HEAD_SIZE = 128
PAIRS_PER_BIN = 4
ROWS = 4
SUB = 4
CHUNKS = 4
GROUPS = 4
SKEW = 0
TASKS = (1, 2, 3, 4)


def iota(shape, dim):
    return lax.broadcasted_iota(jnp.int32, shape, dim)


def split3(x):
    high = x.astype(BF16)
    rest = x - high.astype(F32)
    middle = rest.astype(BF16)
    low = (rest - middle.astype(F32)).astype(BF16)
    return high, middle, low


def left_terms(x):
    high, middle, low = split3(x)
    return jnp.concatenate([high, middle, high, middle, high, low], axis=1)


def right_terms(x):
    high, middle, low = split3(x)
    return jnp.concatenate([high, middle, middle, high, low, high], axis=1)


def product(left, right):
    return lax.dot_general(left, right, (((1,), (1,)), ((), ())), preferred_element_type=F32)


def kernel(
    n, heads, group,
    query, key, value, query_other, key_other, value_other, cotangent, segments, plan, offsets,
    head_out, query_out, kv_out,
    first_kv, first_q, send_kv, send_q, ring_kv, bin_q,
    bias, members, starts_in, part_out, part_in,
    send1, recv1_kv, recv1_q, send2, recv2_kv, recv2_q,
    own_send, own_recv, ring_send, ring_recv, small_send, small_recv,
):
    me = lax.axis_index("dp")
    head = lax.axis_index("head")
    ring = n // SUB
    bins = ring // GROUPS
    width = HEAD_SIZE
    rows = ROWS * n
    rows_here = rows // heads
    per_chunk = group // CHUNKS
    planes = 3 * per_chunk
    share = rows // SUB
    part_rows = share // GROUPS
    ring_rows = SUB * part_rows
    reach = ring // 2
    z, sub = me // SUB, me % SUB
    onward = 1 - 2 * (sub % 2)

    def along(steps):
        return (z + steps + ring) % ring

    barrier = pltpu.get_barrier_semaphore()

    def greet(device):
        pl.semaphore_signal(barrier, inc=1, device_id=device, device_id_type=MESH)

    def greet_head(i, carry):
        greet((me, (head + i) % heads))
        return carry

    def greet_sub(i, carry):
        greet((z * SUB + (sub + i) % SUB, head))
        return carry

    def greet_ring(i, carry):
        greet((along(i) * SUB + sub, head))
        return carry

    lax.fori_loop(1, heads, greet_head, 0)
    lax.fori_loop(1, SUB, greet_sub, 0)
    lax.fori_loop(1, ring, greet_ring, 0)
    pl.semaphore_wait(barrier, heads + SUB + ring - 3)

    def remote(source, target, send, receive, device):
        return pltpu.make_async_remote_copy(
            src_ref=source,
            dst_ref=target,
            send_sem=send,
            recv_sem=receive,
            device_id=device,
            device_id_type=MESH,
        )

    def wait_for(ref, semaphore):
        pltpu.make_async_copy(ref, ref, semaphore).wait()

    def sources(chunk, j):
        if chunk == 0:
            for plane, ref in enumerate((key, key_other, value, value_other)):
                yield ref, pl.multiple_of(j * width, width), plane
        else:
            for place, ref in enumerate((query, query_other, cotangent)):
                for inner in range(per_chunk):
                    at = j * (group * width) + ((chunk - 1) * per_chunk + inner) * width
                    yield ref, pl.multiple_of(at, width), place * per_chunk + inner

    def first_of(chunk):
        return first_kv if chunk == 0 else first_q.at[chunk - 1]

    def start_first(chunk):
        at = pl.multiple_of(head * rows_here, 8)
        for some in range(4 if chunk == 0 else 1):

            def pieces(j):
                for ref, column, plane in sources(chunk, j):
                    if chunk or plane == some:
                        arrived = recv1_q.at[chunk - 1] if chunk else recv1_kv.at[plane]
                        target = first_of(chunk).at[plane, pl.ds(at, rows_here), :]
                        yield ref.at[:, pl.ds(column, width)], target, arrived

            def to(i, carry):
                j = (head + i) % heads
                for source, target, arrived in pieces(j):
                    remote(source, target, send1.at[chunk], arrived, (me, j)).start()
                return carry

            lax.fori_loop(1, heads, to, 0)
            for source, target, arrived in pieces(head):
                pltpu.make_async_copy(source, target, arrived).start()

    def spread(source, target, send, arrived):
        for i in range(1, SUB):
            to = (sub + i) % SUB
            remote(source(to), target, send, arrived, (z * SUB + to, head)).start()
        pltpu.make_async_copy(source(sub), target, arrived).start()

    start_first(0)

    segment = segments[...]
    lane = iota((1, width), 1)
    starts = jnp.zeros((1, width), F32)
    for g in range(1, PAIRS_PER_BIN):
        start = jnp.sum(jnp.where(segment < g, 1.0, 0.0), axis=1, keepdims=True)
        starts = jnp.where(lane == g, start, starts)
    starts_in[z] = jnp.broadcast_to(starts, (8, width))

    def tell(i, carry):
        remote(
            starts_in.at[z], starts_in.at[z], small_send.at[0], small_recv.at[0],
            (along(i) * SUB + sub, head),
        ).start()
        return carry

    lax.fori_loop(1, ring, tell, 0)

    off_row = offsets[...].astype(F32)
    plan_row = plan[...].astype(F32)
    square = (n, n)
    same = iota(square, 0) == iota(square, 1)
    lanes = iota(square, 1).astype(F32)
    off_column = jnp.sum(jnp.where(same, off_row, 0.0), axis=1, keepdims=True)
    plan_column = jnp.sum(jnp.where(same, plan_row, 0.0), axis=1, keepdims=True)
    distance = jnp.sum(jnp.where(plan_column == lanes, off_row, 0.0), axis=1, keepdims=True)
    target = me.astype(F32) + distance
    target = jnp.where(target >= n, target - n, target)
    wide = (n, rows)
    one = (1, rows)
    block = iota(wide, 1) // ROWS
    target_row = jnp.sum(jnp.where(iota(wide, 0) == block, target, 0.0), axis=0, keepdims=True)
    key_in = target_row * ROWS + (iota(one, 1) % ROWS).astype(F32)
    out = iota((rows, 1), 0)
    to_sub, inside = out // share, out % share
    kv_bin = inside // part_rows * bins + inside % bins
    kv_row = inside % part_rows // bins

    def ordering(bin_z, row):
        key_to = ((bin_z * SUB + to_sub) * ROWS + row).astype(F32)
        return jnp.where(key_to == key_in, 1.0, 0.0).astype(BF16)

    def moved(order, block):
        high, middle, low = split3(block)
        result = jnp.dot(order, high, preferred_element_type=F32)
        result += jnp.dot(order, middle, preferred_element_type=F32)
        return result + jnp.dot(order, low, preferred_element_type=F32)

    order_kv = ordering(kv_bin, kv_row)
    order_q = ordering(inside % ring, inside // ring)

    def second_kv(plane):
        wait_for(first_kv.at[plane], recv1_kv.at[plane])
        send_kv[plane] = moved(order_kv, first_kv[plane]).reshape(SUB, GROUPS, part_rows, width)
        at = pl.multiple_of(z * ring_rows + sub * part_rows, 8)
        target = ring_kv.at[:, plane, pl.ds(at, part_rows), :]
        spread(lambda to: send_kv.at[plane, to], target, send2.at[0], recv2_kv.at[plane])

    def second_q(c):
        wait_for(first_q.at[c], recv1_q.at[c])
        for plane in range(0, planes, 2):
            both = jnp.concatenate([first_q[c, plane], first_q[c, plane + 1]], axis=1)
            both = moved(order_q, both)
            send_q[c, plane] = both[:, :width]
            send_q[c, plane + 1] = both[:, width:]
        target = bin_q.at[c, :, pl.ds(pl.multiple_of(sub * share, 8), share), :]
        spread(
            lambda to: send_q.at[c, :, pl.ds(pl.multiple_of(to * share, 8), share), :],
            target, send2.at[c + 1], recv2_q.at[c],
        )

    def plane_of(plane, origin):
        return ring_kv.at[:, plane, pl.ds(pl.multiple_of(origin * ring_rows, 8), ring_rows), :]

    def piece(g, origin):
        return ring_kv.at[g, :, pl.ds(pl.multiple_of(origin * ring_rows, 8), ring_rows), :]

    def turn_of(way):
        return onward * (1 - 2 * way)

    def next_of(way):
        return (along(turn_of(way)) * SUB + sub, head)

    def send_own(plane):
        held = plane_of(plane, z)
        wait_for(held, recv2_kv.at[plane])
        for way in range(2):
            remote(held, held, own_send.at[way], own_recv.at[way, plane], next_of(way)).start()

    def receive_first():
        for way in range(2):
            for plane in range(4):
                wait_for(plane_of(plane, along(-turn_of(way))), own_recv.at[way, plane])

    def ring_step(g, step):
        for way in range(2):
            if step > reach - way:
                continue
            held = piece(g, along(-turn_of(way) * step))
            if step > 1:
                wait_for(held, ring_recv.at[way, g, step - 2])
            if step < reach - way:
                remote(
                    held, held, ring_send.at[way, g], ring_recv.at[way, g, step - 1], next_of(way)
                ).start()

    second_kv(0)
    second_kv(1)
    send_own(0)
    second_kv(2)
    send_own(1)
    second_kv(3)
    start_first(1)
    send_own(2)
    send_own(3)
    start_first(2)

    q_index = iota((SUB * ROWS, 1), 0)
    q_source = z * SUB + q_index // ROWS
    k_source = iota(one, 1) // ROWS

    def describe(at, carry):
        which = at * SUB + sub
        starts = starts_in[at]
        k_distance = ((which - k_source + n) % n).astype(F32)
        k_slot = jnp.sum(
            jnp.where(off_column == k_distance, iota(wide, 0).astype(F32), 0.0), axis=0, keepdims=True
        )
        k_place = k_slot * ROWS + (iota(one, 1) % ROWS).astype(F32)
        q_distance = ((which - q_source + n) % n).astype(F32)
        tall = (SUB * ROWS, n)
        q_slot = jnp.sum(
            jnp.where(off_row == q_distance, iota(tall, 1).astype(F32), 0.0), axis=1, keepdims=True
        )
        q_place = q_slot * ROWS + (q_index % ROWS).astype(F32)
        begin = jnp.zeros_like(q_place)
        k_segment = jnp.zeros_like(k_place)
        for g in range(1, PAIRS_PER_BIN):
            start = starts[:1, g : g + 1]
            begin = jnp.where(q_place >= start, start, begin)
            k_segment += jnp.where(k_place >= start, 1.0, 0.0)
        allowed = jnp.logical_and(k_place <= q_place, k_place >= begin)
        bias[at] = jnp.where(allowed, 0.0, -jnp.inf)
        members[at] = jnp.where(k_segment == iota((8, rows), 0).astype(F32), 1.0, 0.0)
        return carry

    scale = width**-0.5

    def softmax(scores, mask):
        scores = scores * scale + mask
        raised = jnp.exp(scores - jnp.max(scores, axis=1, keepdims=True))
        return raised * (1.0 / jnp.sum(raised, axis=1, keepdims=True))

    def work(at):
        g, inner_bin = at // bins, at % bins

        def keys(plane):
            return ring_kv[g, plane, pl.ds(inner_bin, rows, stride=bins), :]

        def queries(place):
            found = [
                bin_q[i // per_chunk, place * per_chunk + i % per_chunk, pl.ds(at, SUB * ROWS, stride=ring), :]
                for i in range(group)
            ]
            return jnp.concatenate(found, axis=0)

        key_terms = jnp.concatenate([right_terms(keys(0)), right_terms(keys(1))], axis=0)
        value_terms = jnp.concatenate([right_terms(keys(2)), right_terms(keys(3))], axis=0)
        both = jnp.concatenate([left_terms(queries(0)), left_terms(queries(1))], axis=0)
        scores = product(both, key_terms)
        grads = product(left_terms(queries(2)), value_terms)
        count = group * SUB * ROWS
        top, bottom = scores[:count], scores[count:]
        plain = top[:, :rows]
        mask = jnp.concatenate([bias[at]] * group, axis=0)
        weight = softmax(plain, mask)
        weight_other = softmax(bottom[:, rows:], mask)
        part = weight * grads[:, :rows]
        row_dot = jnp.sum(part, axis=1, keepdims=True)
        slope = (part - weight * row_dot) * scale
        head_term = weight_other * grads[:, rows:] - part
        query_term = slope * (bottom[:, :rows] - plain)
        kv_term = slope * (top[:, rows:] - plain) + (weight * grads[:, rows:] - part)
        by_head = (group, SUB * ROWS, rows)
        sums = jnp.concatenate(
            [
                jnp.sum(head_term.reshape(by_head), axis=1),
                jnp.sum(query_term.reshape(by_head), axis=1),
                jnp.sum(kv_term.reshape(-1, 8, rows), axis=0),
            ],
            axis=0,
        )
        found = jnp.zeros((2 * group + 8, width), F32)
        member = members[at]
        for g in range(PAIRS_PER_BIN):
            line = jnp.sum(sums * member[g : g + 1], axis=1, keepdims=True)
            found = jnp.where(lane == g, line, found)
        part_out[at] = found

        @pl.when(at != z)
        def _():
            remote(
                part_out.at[at], part_in.at[z], small_send.at[1], small_recv.at[1], (at * SUB + sub, head)
            ).start()

        @pl.when(at == z)
        def _():
            pltpu.make_async_copy(part_out.at[at], part_in.at[z], small_recv.at[1]).start()

    others = starts_in.at[pl.ds(0, ring - 1)]
    wait_for(others, small_send.at[0])
    wait_for(others, small_recv.at[0])
    lax.fori_loop(0, ring, describe, 0)
    receive_first()
    for tau in range(1, reach):
        for g in range(GROUPS):
            if tau - SKEW * g > 0:
                ring_step(g, tau - SKEW * g)
        for c, when in enumerate(TASKS):
            if tau == when:
                second_q(c)
                if c + 3 <= CHUNKS:
                    start_first(c + 3)
    for c in range(CHUNKS):
        wait_for(bin_q.at[c], recv2_q.at[c])
    done = [reach - 1 - SKEW * g for g in range(GROUPS)]
    for g in range(GROUPS):
        while done[g] < reach:
            for i in range(g, GROUPS if SKEW else g + 1):
                done[i] += 1
                if done[i] > 0:
                    ring_step(i, done[i])

        def one_bin(i, carry):
            work(g * bins + i)
            return carry

        lax.fori_loop(0, bins, one_bin, 0)

    for chunk in range(CHUNKS + 1):
        wait_for(first_of(chunk).at[:, pl.ds(0, (heads - 1) * rows_here), :], send1.at[chunk])
        wait_for(first_of(chunk).at[:, pl.ds(0, (SUB - 1) * share), :], send2.at[chunk])
    for g in range(GROUPS):
        for way in range(2):
            wait_for(ring_kv.at[g, :, pl.ds(0, (reach - way - 1) * ring_rows), :], ring_send.at[way, g])
    for way in range(2):
        wait_for(ring_kv.at[:, :, pl.ds(0, ring_rows), :], own_send.at[way])
    wait_for(part_out.at[pl.ds(0, ring - 1)], small_send.at[1])
    wait_for(part_in, small_recv.at[1])
    total = jnp.sum(part_in[...], axis=0)
    eye = iota((group, group), 0) == iota((group, group), 1)
    for g in range(PAIRS_PER_BIN):
        column = total[:, g : g + 1]
        head_out[g : g + 1, :] = jnp.sum(jnp.where(eye, column[:group], 0.0), axis=0, keepdims=True)
        query_out[g : g + 1, :] = jnp.sum(
            jnp.where(eye, column[group : 2 * group], 0.0), axis=0, keepdims=True
        )
        kv_out[g : g + 1, :] = jnp.sum(column[2 * group :], axis=0, keepdims=True)


def shards(n, heads, *arrays):
    segments, plan, offsets = arrays[7:]
    group = arrays[0].shape[1] // arrays[1].shape[1]
    planes = 3 * group // CHUNKS
    rows = ROWS * n
    ring = n // SUB
    hbm = pl.BlockSpec(memory_space=pltpu.HBM)
    vmem = pl.BlockSpec(memory_space=pltpu.VMEM)
    dma = pltpu.SemaphoreType.DMA
    return pl.pallas_call(
        functools.partial(kernel, n, heads, group),
        out_shape=[
            jax.ShapeDtypeStruct((PAIRS_PER_BIN, group), F32),
            jax.ShapeDtypeStruct((PAIRS_PER_BIN, group), F32),
            jax.ShapeDtypeStruct((PAIRS_PER_BIN, 1), F32),
        ],
        in_specs=[hbm] * 7 + [vmem] * 3,
        out_specs=[vmem] * 3,
        scratch_shapes=[
            pltpu.VMEM((4, rows, HEAD_SIZE), F32),
            pltpu.VMEM((CHUNKS, planes, rows, HEAD_SIZE), F32),
            pltpu.VMEM((4, SUB, GROUPS, rows // SUB // GROUPS, HEAD_SIZE), F32),
            pltpu.VMEM((CHUNKS, planes, rows, HEAD_SIZE), F32),
            pltpu.VMEM((GROUPS, 4, ring * rows // GROUPS, HEAD_SIZE), F32),
            pltpu.VMEM((CHUNKS, planes, rows, HEAD_SIZE), F32),
            pltpu.VMEM((ring, SUB * ROWS, rows), F32),
            pltpu.VMEM((ring, 8, rows), F32),
            pltpu.VMEM((ring, 8, HEAD_SIZE), F32),
            pltpu.VMEM((ring, 2 * group + 8, HEAD_SIZE), F32),
            pltpu.VMEM((ring, 2 * group + 8, HEAD_SIZE), F32),
            dma((CHUNKS + 1,)),
            dma((4,)),
            dma((CHUNKS,)),
            dma((CHUNKS + 1,)),
            dma((4,)),
            dma((CHUNKS,)),
            dma((2,)),
            dma((2, 4)),
            dma((2, GROUPS)),
            dma((2, GROUPS, ring // 2 - 1)),
            dma((2,)),
            dma((2,)),
        ],
        compiler_params=pltpu.CompilerParams(
            collective_id=0, has_side_effects=True, vmem_limit_bytes=60 * 1024 * 1024
        ),
    )(*arrays[:7], segments, plan, offsets.reshape(1, -1))


def solution(mesh):
    rows = P(("dp", "head"), None)
    return jax.shard_map(
        functools.partial(shards, mesh.shape["dp"], mesh.shape["head"]),
        mesh=mesh,
        in_specs=(rows,) * 7 + (P("dp", None), P("dp", None), P()),
        out_specs=(P("dp", "head"),) * 3,
        check_vma=False,
    )
```

time: 156 us -> 134 us (0.86)
  Pallas kernels: 153 us -> 131 us
    pallas_call x1, Pallas kernels: 153 us -> 131 us  [shards(): pl.pallas_call(functools.partial(kernel, n, heads, group), out_shape=[jax...]
where the time goes in v1:
time: 134 us
  Pallas kernels  131 us (98%)
  local copies, waits for them, and re-layouts  2.51 us (2%)
    pallas_call x1, Pallas kernels, shards(): pl.pallas_call(functools.partial(kernel, n, heads, group), out_shape=[jax...  131 us

profile of v1, /device:TPU:1, one launch (start us, length us, event | category | flops | bytes accessed | tf_op | source)
XLA Modules:
  0.0 134.1 jit_solution(7767917714431974882)
XLA Ops:
  0.6 131.0 %shard_map.121 = (f32[4,8]{1,0:T(4,128)}, f32[4,8]{1,0:T(4,128)}, f32[4,1]{1,0:T(4,128)}) custom-call(f32[32,8192]{1,0:T(8,128)} %query.1, f32[32,1024]{1,0:T(8,128)} %key.1, f32[32,1024]{1,0:T(8,128)} %value.1, f32[32,8192]{1,0:T(8,128)} %query_other.1, f32[32,1024]{1,0:T(8,128)} %key_other.1, f32[32,1024]{1,0:T(8,128)} %value_other.1, ...), custom_call_target="tpu_custom_call" | custom-call | tf_op jit(solution)/shard_map/pallas_call | solution.py:422
  131.6 0.0 copy-start
  131.6 0.0 copy-start.2
  131.6 0.7 copy-done
  132.3 0.6 copy.13
  132.9 0.0 copy-done.2
  132.9 0.0 copy-start.1
  132.9 0.6 copy.16
  133.5 0.1 copy-done.1
  133.6 0.6 copy.17
Async XLA Ops:
  131.6 0.7 copy-start
  131.6 1.3 copy-start.2
  132.9 0.7 copy-start.1

commit v2 on v1

--- a/solution.py
+++ b/solution.py
@@ -15,7 +15,7 @@
 ROWS = 4
 SUB = 4
 CHUNKS = 4
-GROUPS = 4
+GROUPS = 8
 SKEW = 0
 TASKS = (1, 2, 3, 4)
 
@@ -49,7 +49,7 @@
 def kernel(
     n, heads, group,
     query, key, value, query_other, key_other, value_other, cotangent, segments, plan, offsets,
-    head_out, query_out, kv_out,
+    out_ref,
     first_kv, first_q, send_kv, send_q, ring_kv, bin_q,
     bias, members, starts_in, part_out, part_in,
     send1, recv1_kv, recv1_q, send2, recv2_kv, recv2_q,
@@ -69,7 +69,6 @@
     ring_rows = SUB * part_rows
     reach = ring // 2
     z, sub = me // SUB, me % SUB
-    onward = 1 - 2 * (sub % 2)
 
     def along(steps):
         return (z + steps + ring) % ring
@@ -228,32 +227,36 @@
         return ring_kv.at[g, :, pl.ds(pl.multiple_of(origin * ring_rows, 8), ring_rows), :]
 
     def turn_of(way):
-        return onward * (1 - 2 * way)
+        return 1 - 2 * way
 
     def next_of(way):
         return (along(turn_of(way)) * SUB + sub, head)
 
     def send_own(plane):
-        held = plane_of(plane, z)
-        wait_for(held, recv2_kv.at[plane])
-        for way in range(2):
-            remote(held, held, own_send.at[way], own_recv.at[way, plane], next_of(way)).start()
+        wait_for(plane_of(plane, z), recv2_kv.at[plane])
+        for place in range(GROUPS if plane == 3 else 1):
+            held = piece(place, z).at[3] if plane == 3 else plane_of(plane, z)
+            for way in range(2):
+                arrived = own_recv.at[way, plane + place]
+                remote(held, held, own_send.at[way], arrived, next_of(way)).start()
 
     def receive_first():
         for way in range(2):
-            for plane in range(4):
+            for plane in range(3):
                 wait_for(plane_of(plane, along(-turn_of(way))), own_recv.at[way, plane])
 
     def ring_step(g, step):
         for way in range(2):
-            if step > reach - way:
-                continue
             held = piece(g, along(-turn_of(way) * step))
-            if step > 1:
-                wait_for(held, ring_recv.at[way, g, step - 2])
-            if step < reach - way:
+            half = held.at[pl.ds(2 * way, 2)]
+            if step == 1:
+                wait_for(held.at[3], own_recv.at[way, 3 + g])
+            else:
+                wait_for(half if step == reach else held, ring_recv.at[way, g, step - 2])
+            if step < reach:
+                going = half if step == reach - 1 else held
                 remote(
-                    held, held, ring_send.at[way, g], ring_recv.at[way, g, step - 1], next_of(way)
+                    going, going, ring_send.at[way, g], ring_recv.at[way, g, step - 1], next_of(way)
                 ).start()
 
     second_kv(0)
@@ -266,6 +269,8 @@
     send_own(2)
     send_own(3)
     start_first(2)
+    start_first(3)
+    start_first(4)
 
     q_index = iota((SUB * ROWS, 1), 0)
     q_source = z * SUB + q_index // ROWS
@@ -371,8 +376,6 @@
         for c, when in enumerate(TASKS):
             if tau == when:
                 second_q(c)
-                if c + 3 <= CHUNKS:
-                    start_first(c + 3)
     for c in range(CHUNKS):
         wait_for(bin_q.at[c], recv2_q.at[c])
     done = [reach - 1 - SKEW * g for g in range(GROUPS)]
@@ -394,20 +397,19 @@
         wait_for(first_of(chunk).at[:, pl.ds(0, (SUB - 1) * share), :], send2.at[chunk])
     for g in range(GROUPS):
         for way in range(2):
-            wait_for(ring_kv.at[g, :, pl.ds(0, (reach - way - 1) * ring_rows), :], ring_send.at[way, g])
+            wait_for(ring_kv.at[g, pl.ds(0, 2), pl.ds(0, (2 * reach - 3) * ring_rows), :], ring_send.at[way, g])
     for way in range(2):
         wait_for(ring_kv.at[:, :, pl.ds(0, ring_rows), :], own_send.at[way])
     wait_for(part_out.at[pl.ds(0, ring - 1)], small_send.at[1])
     wait_for(part_in, small_recv.at[1])
     total = jnp.sum(part_in[...], axis=0)
-    eye = iota((group, group), 0) == iota((group, group), 1)
+    shape = (2 * group + 8, width)
+    eye = iota(shape, 0) == iota(shape, 1)
     for g in range(PAIRS_PER_BIN):
-        column = total[:, g : g + 1]
-        head_out[g : g + 1, :] = jnp.sum(jnp.where(eye, column[:group], 0.0), axis=0, keepdims=True)
-        query_out[g : g + 1, :] = jnp.sum(
-            jnp.where(eye, column[group : 2 * group], 0.0), axis=0, keepdims=True
-        )
-        kv_out[g : g + 1, :] = jnp.sum(column[2 * group :], axis=0, keepdims=True)
+        line = jnp.where(eye, total[:, g : g + 1], 0.0)
+        out_ref[g : g + 1, :] = jnp.sum(line, axis=0, keepdims=True)
+    keyed = jnp.sum(total[2 * group :], axis=0, keepdims=True)
+    out_ref[PAIRS_PER_BIN:, :] = jnp.broadcast_to(keyed, (8 - PAIRS_PER_BIN, width))
 
 
 def shards(n, heads, *arrays):
@@ -419,15 +421,11 @@
     hbm = pl.BlockSpec(memory_space=pltpu.HBM)
     vmem = pl.BlockSpec(memory_space=pltpu.VMEM)
     dma = pltpu.SemaphoreType.DMA
-    return pl.pallas_call(
+    packed = pl.pallas_call(
         functools.partial(kernel, n, heads, group),
-        out_shape=[
-            jax.ShapeDtypeStruct((PAIRS_PER_BIN, group), F32),
-            jax.ShapeDtypeStruct((PAIRS_PER_BIN, group), F32),
-            jax.ShapeDtypeStruct((PAIRS_PER_BIN, 1), F32),
-        ],
+        out_shape=jax.ShapeDtypeStruct((8, HEAD_SIZE), F32),
         in_specs=[hbm] * 7 + [vmem] * 3,
-        out_specs=[vmem] * 3,
+        out_specs=vmem,
         scratch_shapes=[
             pltpu.VMEM((4, rows, HEAD_SIZE), F32),
             pltpu.VMEM((CHUNKS, planes, rows, HEAD_SIZE), F32),
@@ -447,7 +445,7 @@
             dma((4,)),
             dma((CHUNKS,)),
             dma((2,)),
-            dma((2, 4)),
+            dma((2, 3 + GROUPS)),
             dma((2, GROUPS)),
             dma((2, GROUPS, ring // 2 - 1)),
             dma((2,)),
@@ -457,6 +455,9 @@
             collective_id=0, has_side_effects=True, vmem_limit_bytes=60 * 1024 * 1024
         ),
     )(*arrays[:7], segments, plan, offsets.reshape(1, -1))
+    found = packed[:PAIRS_PER_BIN]
+    keyed = packed[PAIRS_PER_BIN : PAIRS_PER_BIN + 1, :PAIRS_PER_BIN]
+    return found[:, :group], found[:, group : 2 * group], keyed.reshape(-1, 1)
 
 
 def solution(mesh):

time: 134 us -> 132 us (0.985)
  the two profiles are of different devices: /device:TPU:1 before, /device:TPU:3 now
where the time goes in v2:
time: 132 us
  Pallas kernels  129 us (98%)
  local copies, waits for them, and re-layouts  2.58 us (2%)
    pallas_call x1, Pallas kernels, shards(): pl.pallas_call(functools.partial(kernel, n, heads, group), out_shape=jax....  129 us

profile of v2, /device:TPU:3, one launch (start us, length us, event | category | flops | bytes accessed | tf_op | source)
XLA Modules:
  0.0 131.9 jit_solution(368146627030283273)
XLA Ops:
  0.6 128.6 %shard_map.121 = f32[8,128]{1,0:T(8,128)} custom-call(f32[32,8192]{1,0:T(8,128)} %query.1, f32[32,1024]{1,0:T(8,128)} %key.1, f32[32,1024]{1,0:T(8,128)} %value.1, f32[32,8192]{1,0:T(8,128)} %query_other.1, f32[32,1024]{1,0:T(8,128)} %key_other.1, f32[32,1024]{1,0:T(8,128)} %value_other.1, f32[32,8192]{1,0:T(8,128)} %cotangent.1, s32[1,256]{1,0:T(1,128)} %segments.1, ...), custom_call_target="tpu_custom_call" | custom-call | tf_op jit(solution)/shard_map/pallas_call | solution.py:424
  129.3 1.4 %fusion = (f32[4,8]{1,0:T(4,128)}, f32[4,8]{1,0:T(4,128)}) fusion(f32[8,128]{1,0:T(8,128)} %shard_map.121), kind=kLoop, calls=%fused_computation.1 | loop fusion | bytes 512 | tf_op jit(solution)/shard_map/slice | solution.py:460
  130.7 1.2 slice_bitcast_fusion

commit v3 on v2

--- a/solution.py
+++ b/solution.py
@@ -268,9 +268,6 @@
     start_first(1)
     send_own(2)
     send_own(3)
-    start_first(2)
-    start_first(3)
-    start_first(4)
 
     q_index = iota((SUB * ROWS, 1), 0)
     q_source = z * SUB + q_index // ROWS
@@ -365,14 +362,18 @@
             pltpu.make_async_copy(part_out.at[at], part_in.at[z], small_recv.at[1]).start()
 
     others = starts_in.at[pl.ds(0, ring - 1)]
-    wait_for(others, small_send.at[0])
-    wait_for(others, small_recv.at[0])
-    lax.fori_loop(0, ring, describe, 0)
     receive_first()
     for tau in range(1, reach):
         for g in range(GROUPS):
             if tau - SKEW * g > 0:
                 ring_step(g, tau - SKEW * g)
+        if tau == 1:
+            start_first(2)
+            start_first(3)
+            start_first(4)
+            wait_for(others, small_send.at[0])
+            wait_for(others, small_recv.at[0])
+            lax.fori_loop(0, ring, describe, 0)
         for c, when in enumerate(TASKS):
             if tau == when:
                 second_q(c)

time: 132 us -> 132 us (level)
  the two profiles are of different devices: /device:TPU:3 before, /device:TPU:8 now
where the time goes in v3:
time: 132 us; the launch traced here: 131 us
  Pallas kernels  128 us (97%)
  local copies, waits for them, and re-layouts  2.58 us (2%)
    pallas_call x1, Pallas kernels, shards(): pl.pallas_call(functools.partial(kernel, n, heads, group), out_shape=jax....  128 us

profile of v3, /device:TPU:8, one launch (start us, length us, event | category | flops | bytes accessed | tf_op | source)
XLA Modules:
  0.0 131.3 jit_solution(9128890348922946662)
XLA Ops:
  0.6 128.1 %shard_map.121 = f32[8,128]{1,0:T(8,128)} custom-call(f32[32,8192]{1,0:T(8,128)} %query.1, f32[32,1024]{1,0:T(8,128)} %key.1, f32[32,1024]{1,0:T(8,128)} %value.1, f32[32,8192]{1,0:T(8,128)} %query_other.1, f32[32,1024]{1,0:T(8,128)} %key_other.1, f32[32,1024]{1,0:T(8,128)} %value_other.1, f32[32,8192]{1,0:T(8,128)} %cotangent.1, s32[1,256]{1,0:T(1,128)} %segments.1, ...), custom_call_target="tpu_custom_call" | custom-call | tf_op jit(solution)/shard_map/pallas_call | solution.py:425
  128.7 1.4 %fusion = (f32[4,8]{1,0:T(4,128)}, f32[4,8]{1,0:T(4,128)}) fusion(f32[8,128]{1,0:T(8,128)} %shard_map.121), kind=kLoop, calls=%fused_computation.1 | loop fusion | bytes 512 | tf_op jit(solution)/shard_map/slice | solution.py:461
  130.1 1.2 slice_bitcast_fusion
